TPU v7x, 256 devices: a whole 4x4x8 slice. The times are simulated.
256 devices in a mesh: dp: 16 (over z, core), tensor: 16 (over y, x).
Axes of the slice: x: 4, y: 4, z: 8, core: 2. Of those that a mesh axis runs over, the one named last changes fastest.
Arguments:
- tokens: bfloat16 [8192, 8192], P('dp', 'tensor'), may hold values from -6 to 6
- grad_out: bfloat16 [8192, 28672], P('dp', 'tensor'), may hold values from -0.06591797 to 0.06591797
- projector: bfloat16 [8192, 1024], P('tensor'), may hold values from -0.1875 to 0.1875
- weight: float32 [8192, 28672], P('dp', 'tensor'), may hold values from -6 to 6
- first_moment: float32 [1024, 28672], P('dp', 'tensor'), may hold values from -6 to 6
- second_moment: float32 [1024, 28672], P('dp', 'tensor'), may hold values from 0.5 to 4
Outputs:
- new_weight: float32 [8192, 28672], P('dp', 'tensor')
- new_first: float32 [1024, 28672], P('dp', 'tensor')
- new_second: float32 [1024, 28672], P('dp', 'tensor')
All inputs are finite; a program needn't handle non-finite values.
Results may differ from a plain program's by a relative error of at most 0.00098.
Values may be sent and summed in bfloat16 or wider, within the bound.
A program may use at most 64 MiB of HBM per device.

v0:
```python
import jax
import jax.numpy as jnp
from jax import lax
from jax.sharding import PartitionSpec as P

STEP = 1000


def spread(value, axis, source):
    kept = jnp.where(lax.axis_index(axis) == source, value, 0).astype(value.dtype)
    return lax.psum(kept, axis)


def on_device(tokens, grad_out, projector, weight, first_moment, second_moment):
    partial_value = jnp.dot(tokens, projector, preferred_element_type=jnp.float32)
    projected = lax.psum(partial_value, "tensor").astype(jnp.bfloat16)
    grad_share = lax.psum_scatter(
        lax.dot_general(
            projected, grad_out, (((0,), (0,)), ((), ())), preferred_element_type=jnp.float32
        ),
        "dp",
        scatter_dimension=0,
        tiled=True,
    )
    new_first = 0.9 * first_moment + 0.1 * grad_share
    new_second = 0.999 * second_moment + 0.001 * grad_share * grad_share
    first_fix = 1.0 - 0.9**STEP
    second_fix = 1.0 - 0.999**STEP
    direction = (new_first / first_fix / (jnp.sqrt(new_second / second_fix) + 1e-08)).astype(
        jnp.bfloat16
    )
    whole_direction = lax.all_gather(direction, "dp", axis=0, tiled=True)
    weight_rows = weight.shape[0]
    holder_rows = projector.shape[0]
    first_row = lax.axis_index("dp") * weight_rows
    holder = first_row // holder_rows
    held_block = spread(projector, "tensor", holder)
    new_weight = weight - 0.5 * jnp.dot(
        held_block, whole_direction, preferred_element_type=jnp.float32
    )
    return (new_weight, new_first, new_second)


def solution(mesh):
    in_specs = (
        P("dp", "tensor"),
        P("dp", "tensor"),
        P("tensor", None),
        P("dp", "tensor"),
        P("dp", "tensor"),
        P("dp", "tensor"),
    )
    out_specs = (P("dp", "tensor"), P("dp", "tensor"), P("dp", "tensor"))
    return jax.shard_map(
        on_device, mesh=mesh, in_specs=in_specs, out_specs=out_specs, check_vma=False
    )
```

profile of v0, /device:TPU:1, one launch (start us, length us, event | category | flops | bytes accessed | tf_op | source)
XLA Modules:
  0.0 236.0 jit_solution(11256144189807236220)
XLA Ops:
  8.0 0.0 copy-start
  8.0 0.0 reduce-scatter.2.cloned.1.call-start
  8.1 3.5 %fusion.4 = f32[512,1024]{1,0:T(8,128)} fusion(bf16[512,512]{1,0:T(8,128)(2,1)} %param.6, bf16[512,1024]{1,0:T(8,128)(2,1)} %param.8), kind=kOutput, calls=%fused_computation.8 | convolution fusion | flops 536870912 | bytes 3670016 | tf_op jit(solution)/shard_map/dot_general | solution.py:15
  11.6 82.0 %all-reduce.4 = bf16[512,1024]{1,0:T(8,128)(2,1)S(1)} all-reduce(f32[512,1024]{1,0:T(8,128)} %fusion.4), channel_id=1, replica_groups=mesh['dp'=16,'tensor'=16] {'tensor'}, use_global_device_ids=true, to_apply=%region_1.0 | all-reduce | flops 524288 | bytes 3145728 | tf_op jit(solution)/shard_map/psum | solution.py:16
  93.6 0.0 copy-done
  93.6 5.1 %fusion.5 = f32[1024,1792]{1,0:T(8,128)} fusion(bf16[512,1024]{1,0:T(8,128)(2,1)S(1)} %all-reduce.4, bf16[512,1792]{1,0:T(8,128)(2,1)S(1)} %copy-done), kind=kOutput, calls=%fused_computation.9 | convolution fusion | flops 1879048192 | bytes 10223616 | tf_op jit(solution)/shard_map/dot_general | solution.py:18
  98.6 0.0 copy-start.1
  98.6 0.0 copy-start.2
  98.7 0.0 reduce-scatter.2.cloned.1.call-update
  98.7 0.0 all-reduce.3.cloned.1.call-start
  98.7 1.1 copy-done.1
  99.9 1.0 broadcast_select_fusion
  100.9 0.0 all-reduce.3.cloned.1.call-update
  100.9 0.0 all-gather.2.cloned.1.call-start
  101.0 74.5 %reduce-scatter.2.cloned.1.call-done = f32[64,1792]{1,0:T(8,128)} async-done(((f32[1024,1792]{1,0:T(8,128)}), f32[64,1792]{1,0:T(8,128)}) %reduce-scatter.2.cloned.1.call-update) | async-done | bytes 458768 | tf_op jit(solution)/shard_map/reduce_scatter | solution.py:17
  175.5 0.0 copy-done.2
  175.5 2.3 divide_convert_fusion
  177.8 0.0 all-gather.2.cloned.1.call-update
  177.9 30.5 %all-reduce.3.cloned.1.call-done = bf16[512,1024]{1,0:T(8,128)(2,1)} async-done(((bf16[512,1024]{1,0:T(8,128)(2,1)}), bf16[512,1024]{1,0:T(8,128)(2,1)}) %all-reduce.3.cloned.1.call-update) | async-done | bytes 1048592 | tf_op jit(solution)/shard_map/psum | solution.py:11
  208.3 12.9 %all-gather.2.cloned.1.call-done = bf16[1024,1792]{1,0:T(8,128)(2,1)} async-done(((bf16[64,1792]{1,0:T(8,128)(2,1)}), bf16[1024,1792]{1,0:T(8,128)(2,1)}) %all-gather.2.cloned.1.call-update) | async-done | bytes 3670032 | tf_op jit(solution)/shard_map/all_gather | solution.py:32
  221.2 7.4 %multiply_subtract_fusion = f32[512,1792]{1,0:T(8,128)} fusion(f32[512,1792]{1,0:T(8,128)} %param.9, bf16[512,1024]{1,0:T(8,128)(2,1)} %all-reduce.3.cloned.1.call-done, bf16[1024,1792]{1,0:T(8,128)(2,1)} %all-gather.2.cloned.1.call-done), kind=kOutput, calls=%fused_computation | convolution fusion | flops 1880883200 | bytes 12058624 | tf_op jit(solution)/shard_map/dot_general | solution.py:38
Async XLA Ops:
  8.0 85.6 %copy-start = (bf16[512,1792]{1,0:T(8,128)(2,1)S(1)}, bf16[512,1792]{1,0:T(8,128)(2,1)}, u32[]{:S(2)}) copy-start(bf16[512,1792]{1,0:T(8,128)(2,1)} %param.7) | copy-start | bytes 5505028
  8.0 167.5 %reduce-scatter.2.cloned.1.call-start = ((), (), s32[]{:S(2)}) async-start(), calls=%async_computation.2 | async-start | bytes 7798784 | tf_op jit(solution)/shard_map/reduce_scatter | solution.py:17
  98.6 1.2 copy-start.1
  98.6 76.9 %copy-start.2 = (f32[64,1792]{1,0:T(8,128)S(1)}, f32[64,1792]{1,0:T(8,128)}, u32[]{:S(2)}) copy-start(f32[64,1792]{1,0:T(8,128)} %param.11) | copy-start | bytes 1376260
  98.7 109.6 %all-reduce.3.cloned.1.call-start = ((), (), s32[]{:S(2)}) async-start(), calls=%async_computation.1 | async-start | bytes 2097152 | tf_op jit(solution)/shard_map/psum | solution.py:11
  100.9 120.3 %all-gather.2.cloned.1.call-start = ((), (), s32[]{:S(2)}) async-start(), calls=%async_computation.3 | async-start | bytes 3899392 | tf_op jit(solution)/shard_map/all_gather | solution.py:32
Sparse Core Ops, SparseCore 0:
  98.8 76.6 reduce-scatter.1
  178.0 43.1 all-gather.1
Sparse Core Ops, SparseCore 1:
  103.0 105.3 all-reduce.2
where the time goes:
time: 236 us
  waiting for transfers between devices  118 us (50%)
  blocking collectives  82 us (35%)
  matrix products  16 us (7%)
  between operations  15.5 us (7%)
  other arithmetic  3.34 us (1%)
    psum x1, blocking collectives, on_device(): projected = lax.psum(partial_value, 'tensor').astype(jnp.bfloat16)  82 us
    reduce_scatter x1, waiting for transfers between devices, on_device(): lax.psum_scatter(lax.dot_general(projected, grad_out, (((0,), (0,)), ((),...  74.5 us
    psum x1, waiting for transfers between devices, spread(): return lax.psum(kept, axis)  30.5 us
    all_gather x1, waiting for transfers between devices, on_device(): whole_direction = lax.all_gather(direction, 'dp', axis=0, tiled=True)  12.9 us
    dot_general x1, matrix products, on_device(): jnp.dot(held_block, whole_direction, preferred_element_type=jnp.float32)  7.37 us
    dot_general x1, matrix products, on_device(): lax.dot_general(projected, grad_out, (((0,), (0,)), ((), ())), preferred_...  5.06 us
  transfers between devices with their start and end apart: 3, of which 3 were waited for; matrix products, arithmetic and copies ran while one was open for 1% of the time, Pallas kernels for 0%

commit v1 on v0

v1 whole, which is shorter than its diff:
```python
import functools

import jax
import jax.numpy as jnp
from jax import lax
from jax.experimental import pallas as pl
from jax.experimental.pallas import tpu as pltpu
from jax.sharding import PartitionSpec as P

STEP = 1000
MESH = pl.DeviceIdType.MESH
F32, BF16 = jnp.float32, jnp.bfloat16
K = 4
NZ, NY, NX = 8, 4, 4
ROWS = 64
RB = ROWS // K
NR = NZ * RB
FFL = 1792
HALF = FFL // 2
TILE = 256
OFFSET = 2
PEERS = NY * NX


def kernel(
    tokens, grad_out, projector, weight, first, second,
    out_w, out_first, out_second,
    tok_v, go_v, proj_v, first_v, second_v, pick, pc, part, r1, s1, r2, pj, pjt, gp,
    zs, zr, dir_v, held, hp,
    load_sem, tok_sem, go_sem, x1_sem, x2_sem, pg_sem, z_sem, a_sem, sib_sem, sc_sem, hg_sem,
):
    dp, t = lax.axis_index("dp"), lax.axis_index("tensor")
    z, c = dp // 2, dp % 2
    y, x = t // NX, t % NX

    def at(dz=0, dy=0, dx=0):
        return (lax.rem(z + dz + NZ, NZ) * 2 + c, lax.rem(y + dy, NY) * NX + lax.rem(x + dx, NX))

    sibling = (2 * z + 1 - c, t)

    def plane_peer(j):
        return at(0, j // NX, j % NX)

    def remote(src, dst, sems, idx, device):
        send, recv = sems
        return pltpu.make_async_remote_copy(
            src_ref=src, dst_ref=dst, send_sem=send.at[idx], recv_sem=recv.at[idx],
            device_id=device, device_id_type=MESH,
        )

    barrier = pltpu.get_barrier_semaphore()
    for dz in (1, -1):
        pl.semaphore_signal(barrier, inc=1, device_id=at(dz), device_id_type=MESH)
    pl.semaphore_signal(barrier, inc=1, device_id=sibling, device_id_type=MESH)

    @pl.loop(1, PEERS)
    def _(j):
        pl.semaphore_signal(barrier, inc=1, device_id=plane_peer(j), device_id_type=MESH)

    loads = [
        pltpu.make_async_copy(projector, proj_v, load_sem.at[0]),
        pltpu.make_async_copy(tokens, tok_v.at[c], load_sem.at[1]),
        pltpu.make_async_copy(grad_out, go_v.at[:, c], load_sem.at[2]),
        pltpu.make_async_copy(first, first_v, load_sem.at[3]),
        pltpu.make_async_copy(second, second_v, load_sem.at[4]),
        pltpu.make_async_copy(weight, out_w, load_sem.at[5]),
    ]
    for copy in loads:
        copy.start()

    @pl.loop(0, NZ)
    def _(b):
        row = lax.broadcasted_iota(jnp.int32, (2 * ROWS, K * NR), 0)
        col = lax.broadcasted_iota(jnp.int32, (2 * ROWS, K * NR), 1)
        chunk, in_chunk = col // NR, col % NR
        plane, r = in_chunk // RB, in_chunk % RB
        for cc in range(2):
            hit = (plane == b) & (row == cc * ROWS + chunk * RB + r)
            pick[cc, pl.ds(pl.multiple_of(b * 2 * ROWS, 2 * ROWS), 2 * ROWS), :] = jnp.where(
                hit, 1.0, 0.0
            ).astype(BF16)

    loads[0].wait()
    pc[...] = jnp.dot(proj_v[...], pick[c], preferred_element_type=F32).astype(BF16)
    loads[1].wait()

    def partial_product(h):
        @pl.loop(0, NY)
        def _(yy):
            rows = pl.ds(pl.multiple_of(yy * 128, 128), 128)
            value = jnp.dot(tok_v[h, rows, :], pc[...], preferred_element_type=F32)
            for k in range(K):
                part[k, h, yy] = value[:, k * NR : (k + 1) * NR].reshape(NX, 32, NR)

    partial_product(c)

    pl.semaphore_wait(barrier, 2 + 1 + PEERS - 1)
    tok_copy = remote(tok_v.at[c], tok_v.at[c], tok_sem, 0, sibling)
    go_copy = remote(grad_out, go_v.at[:, c], go_sem, 0, sibling)
    tok_copy.start()
    go_copy.start()

    def x1(k, h, i):
        if h == 0:
            return remote(
                part.at[k, 0, :, lax.rem(x + i, NX)], r1.at[k, 0, i - 1], x1_sem,
                (k * 2 + h) * 3 + i - 1, at(0, 0, i),
            )
        return remote(
            part.at[k, 1, lax.rem(y + i, NY)], r1.at[k, 1, i - 1], x1_sem,
            (k * 2 + h) * 3 + i - 1, at(0, i, 0),
        )

    def x2(k, h, i):
        if h == 0:
            return remote(
                s1.at[k, 0, lax.rem(y + i, NY)], r2.at[k, 0, i - 1], x2_sem,
                (k * 2 + h) * 3 + i - 1, at(0, i, 0),
            )
        return remote(
            s1.at[k, 1, lax.rem(x + i, NX)], r2.at[k, 1, i - 1], x2_sem,
            (k * 2 + h) * 3 + i - 1, at(0, 0, i),
        )

    def plane_gather(k, j):
        return remote(pj.at[k, t], pj.at[k, t], pg_sem, k * PEERS + j, plane_peer(j))

    def z_step(k, d, s):
        cols = pl.ds(d * HALF, HALF) if s == 0 else pl.ds(0, FFL)
        return remote(
            zs.at[k, d, s, :, cols], zr.at[k, d, s, :, cols], z_sem, (k * 2 + d) * 4 + s,
            at(1 if d == 0 else -1),
        )

    def a_step(k, d, s):
        piece = lax.rem(z + (NZ - s if d == 0 else s), NZ)
        cols = pl.ds(d * HALF, HALF) if s == 3 else pl.ds(0, FFL)
        ref = dir_v.at[k, c, piece, :, cols]
        return remote(ref, ref, a_sem, (k * 2 + d) * 4 + s, at(1 if d == 0 else -1))

    def sib(k, n):
        ref = dir_v.at[k, c, lax.rem(z + NZ - n, NZ)]
        return remote(ref, ref, sib_sem, k * NZ + n, sibling)

    def stage_x1(k):
        for h in range(2):
            for i in (1, 2, 3):
                x1(k, h, i).start()

    def stage_x2(k):
        for h in range(2):
            for i in (1, 2, 3):
                x1(k, h, i).wait_recv()
            own = part[k, 0, :, pl.ds(x, 1)].reshape(NY, 32, NR) if h == 0 else part[k, 1, y]
            s1[k, h] = own + r1[k, h, 0] + r1[k, h, 1] + r1[k, h, 2]
            for i in (1, 2, 3):
                x2(k, h, i).start()

    def stage_pg(k):
        for h in range(2):
            for i in (1, 2, 3):
                x2(k, h, i).wait_recv()
            own = s1[k, h, y if h == 0 else x]
            pj[k, t, h] = (own + r2[k, h, 0] + r2[k, h, 1] + r2[k, h, 2]).astype(BF16)

        @pl.loop(1, PEERS)
        def _(j):
            plane_gather(k, j).start()

    def stage_grad(k):
        @pl.loop(1, PEERS)
        def _(j):
            plane_gather(k, j).wait_recv()

        if k == 0:
            loads[2].wait()
            go_copy.wait_recv()
        pjt[...] = pj[k].reshape(PEERS * 64, NR).T

        @pl.loop(0, FFL // TILE)
        def _(n):
            cols = pl.ds(pl.multiple_of(n * TILE, TILE), TILE)
            value = jnp.dot(
                pjt[...], go_v[:, :, :, cols].reshape(PEERS * 64, TILE), preferred_element_type=F32
            )
            gp[k, :, :, cols] = value.reshape(NZ, RB, TILE)

        for d in range(2):
            far = lax.rem(z + 4, NZ)
            cols = slice(d * HALF, (d + 1) * HALF)
            zs[k, d, 0, :, cols] = gp[k, far, :, cols].astype(BF16)
            z_step(k, d, 0).start()

    def stage_z(k, s):
        for d in range(2):
            z_step(k, d, s - 1).wait_recv()
            dest = lax.rem(z + (4 - s if d == 0 else NZ - 4 + s), NZ)
            if s == 1:
                got = slice(d * HALF, (d + 1) * HALF)
                rest = slice((1 - d) * HALF, (2 - d) * HALF)
                zs[k, d, 1, :, got] = (
                    gp[k, dest, :, got] + zr[k, d, 0, :, got].astype(F32)
                ).astype(BF16)
                zs[k, d, 1, :, rest] = gp[k, dest, :, rest].astype(BF16)
            else:
                zs[k, d, s] = (gp[k, dest] + zr[k, d, s - 1].astype(F32)).astype(BF16)
            z_step(k, d, s).start()

    def stage_adam(k):
        for d in range(2):
            z_step(k, d, 3).wait_recv()
        if k == 0:
            loads[3].wait()
            loads[4].wait()
        rows = slice(k * RB, (k + 1) * RB)
        grad = gp[k, z] + zr[k, 0, 3].astype(F32) + zr[k, 1, 3].astype(F32)
        new_first = 0.9 * first_v[rows, :] + 0.1 * grad
        new_second = 0.999 * second_v[rows, :] + 0.001 * grad * grad
        out_first[rows, :] = new_first
        out_second[rows, :] = new_second
        first_fix = 1.0 - 0.9**STEP
        second_fix = 1.0 - 0.999**STEP
        dir_v[k, c, z] = (
            new_first / first_fix / (jnp.sqrt(new_second / second_fix) + 1e-08)
        ).astype(BF16)
        for d in range(2):
            a_step(k, d, 0).start()
        sib(k, 0).start()

    def stage_a(k, s):
        for d in range(2):
            a_step(k, d, s - 1).wait_recv()
            a_step(k, d, s).start()
            sib(k, s if d == 0 else NZ - s).start()

    def stage_last(k):
        for d in range(2):
            a_step(k, d, 3).wait_recv()
        sib(k, 4).start()

    def stage_product(k):
        for n in range(NZ):
            sib(k, n).wait_recv()

        @pl.loop(0, FFL // TILE)
        def _(n):
            cols = pl.ds(pl.multiple_of(n * TILE, TILE), TILE)
            value = jnp.dot(
                hp[:, k * 2 * NR : (k + 1) * 2 * NR],
                dir_v[k, :, :, :, cols].reshape(2 * NR, TILE),
                preferred_element_type=F32,
            )
            out_w[:, cols] = out_w[:, cols] - 0.5 * value

    holder = dp
    is_holder = t == holder

    def piece_of(ref, p):
        return ref.at[pl.ds(pl.multiple_of(p * 32, 32), 32)]

    def scatter(p):
        return pltpu.make_async_remote_copy(
            src_ref=piece_of(proj_v, p), dst_ref=piece_of(held, p),
            send_sem=sc_sem[0].at[p], recv_sem=sc_sem[1].at[0],
            device_id=(dp, p), device_id_type=MESH,
        )

    def held_gather(j):
        return remote(piece_of(held, t), piece_of(held, t), hg_sem, j, plane_peer(j))

    def own_held():
        return pltpu.make_async_copy(proj_v, held, load_sem.at[6])

    def stage_scatter():
        @pl.when(is_holder)
        def _():
            own_held().start()

            @pl.loop(1, PEERS)
            def _(j):
                scatter(lax.rem(t + j, PEERS)).start()

    def stage_held_gather():
        @pl.when(is_holder)
        def _():
            own_held().wait()

        @pl.when(jnp.logical_not(is_holder))
        def _():
            scatter(t).wait_recv()

        @pl.loop(1, PEERS)
        def _(j):
            @pl.when(plane_peer(j)[1] != holder)
            def _():
                held_gather(j).start()

    def stage_held():
        @pl.when(jnp.logical_not(is_holder))
        def _():
            @pl.loop(1, PEERS)
            def _(j):
                held_gather(j).wait_recv()

        for cc in range(2):
            @pl.loop(0, 4)
            def _(b):
                rows = pl.ds(pl.multiple_of(b * 128, 128), 128)
                value = jnp.dot(held[rows, :], pick[cc], preferred_element_type=F32).astype(BF16)
                for k in range(K):
                    lo = (k * 2 + cc) * NR
                    hp[rows, lo : lo + NR] = value[:, k * NR : (k + 1) * NR]

        loads[5].wait()

    tok_copy.wait_recv()
    partial_product(1 - c)

    stages = [
        stage_x1, stage_x2, stage_pg, stage_grad,
        functools.partial(lambda s, k: stage_z(k, s), 1),
        functools.partial(lambda s, k: stage_z(k, s), 2),
        functools.partial(lambda s, k: stage_z(k, s), 3),
        stage_adam,
        functools.partial(lambda s, k: stage_a(k, s), 1),
        functools.partial(lambda s, k: stage_a(k, s), 2),
        functools.partial(lambda s, k: stage_a(k, s), 3),
        stage_last, stage_product,
    ]
    for slot in range(len(stages) + OFFSET * (K - 1)):
        if slot == 5:
            stage_scatter()
        if slot == 8:
            stage_held_gather()
        if slot == 11:
            stage_held()
        for k in range(K):
            n = slot - OFFSET * k
            if 0 <= n < len(stages):
                stages[n](k)

    tok_copy.wait_send()
    go_copy.wait_send()
    for k in range(K):
        for h in range(2):
            for i in (1, 2, 3):
                x1(k, h, i).wait_send()
                x2(k, h, i).wait_send()
            for s in range(4):
                z_step(k, h, s).wait_send()
                a_step(k, h, s).wait_send()
        for n in range(NZ):
            sib(k, n).wait_send()

        @pl.loop(1, PEERS)
        def _(j):
            plane_gather(k, j).wait_send()

    @pl.loop(1, PEERS)
    def _(j):
        @pl.when(plane_peer(j)[1] != holder)
        def _():
            held_gather(j).wait_send()

    @pl.when(is_holder)
    def _():
        @pl.loop(1, PEERS)
        def _(j):
            scatter(lax.rem(t + j, PEERS)).wait_send()


def on_device(tokens, grad_out, projector, weight, first_moment, second_moment):
    dma = pltpu.SemaphoreType.DMA

    def pair(n):
        return [dma((n,)), dma((n,))]

    scratch = [
        pltpu.VMEM((2, 512, 512), BF16),
        pltpu.VMEM((PEERS, 2, 32, FFL), BF16),
        pltpu.VMEM((512, 1024), BF16),
        pltpu.VMEM((ROWS, FFL), F32),
        pltpu.VMEM((ROWS, FFL), F32),
        pltpu.VMEM((2, 1024, K * NR), BF16),
        pltpu.VMEM((512, K * NR), BF16),
        pltpu.VMEM((K, 2, NY, NX, 32, NR), F32),
        pltpu.VMEM((K, 2, 3, 4, 32, NR), F32),
        pltpu.VMEM((K, 2, 4, 32, NR), F32),
        pltpu.VMEM((K, 2, 3, 32, NR), F32),
        pltpu.VMEM((K, PEERS, 2, 32, NR), BF16),
        pltpu.VMEM((NR, PEERS * 64), BF16),
        pltpu.VMEM((K, NZ, RB, FFL), F32),
        pltpu.VMEM((K, 2, 4, RB, FFL), BF16),
        pltpu.VMEM((K, 2, 4, RB, FFL), BF16),
        pltpu.VMEM((K, 2, NZ, RB, FFL), BF16),
        pltpu.VMEM((512, 1024), BF16),
        pltpu.VMEM((512, 1024), BF16),
        dma((7,)),
        pair(1), pair(1), pair(K * 6), pair(K * 6), pair(K * PEERS), pair(K * 8), pair(K * 8),
        pair(K * NZ), pair(PEERS), pair(PEERS),
    ]
    any_spec = pl.BlockSpec(memory_space=pl.ANY)
    vmem_spec = pl.BlockSpec(memory_space=pltpu.VMEM)
    return pl.pallas_call(
        kernel,
        out_shape=(
            jax.ShapeDtypeStruct(weight.shape, F32),
            jax.ShapeDtypeStruct(first_moment.shape, F32),
            jax.ShapeDtypeStruct(second_moment.shape, F32),
        ),
        in_specs=[any_spec] * 6,
        out_specs=[vmem_spec] * 3,
        scratch_shapes=scratch,
        compiler_params=pltpu.CompilerParams(
            collective_id=0, has_side_effects=True, vmem_limit_bytes=56 * 2**20
        ),
        cost_estimate=pl.CostEstimate(
            flops=6 * 10**9, bytes_accessed=13 * 2**20, transcendentals=0
        ),
    )(tokens, grad_out.reshape(PEERS, 32, FFL), projector, weight, first_moment, second_moment)


def solution(mesh):
    spec = P("dp", "tensor")
    in_specs = (spec, spec, P("tensor", None), spec, spec, spec)
    return jax.shard_map(
        on_device, mesh=mesh, in_specs=in_specs, out_specs=(spec, spec, spec), check_vma=False
    )
```

time: 236 us -> 121 us (0.51)
  waiting for transfers between devices: 118 us -> 0 us
  Pallas kernels: 0 us -> 114 us
  blocking collectives: 82 us -> 0 us
  matrix products: 16 us -> 0 us
  between operations: 15.5 us -> 0.66 us
  local copies, waits for them, and re-layouts: 1.14 us -> 5.73 us
  other arithmetic: 3.34 us -> 0 us
    pallas_call x0 -> x1, Pallas kernels: none -> 114 us  [on_device(): pl.pallas_call(kernel, out_shape=(jax.ShapeDtypeStruct(weight.shape, F32)...]
    psum x1 -> x0, blocking collectives: 82 us -> none  [on_device(): projected = lax.psum(partial_value, 'tensor').astype(jnp.bfloat16)]
    reduce_scatter x1 -> x0, waiting for transfers between devices: 74.5 us -> none  [on_device(): lax.psum_scatter(lax.dot_general(projected, grad_out, (((0,), (0,)), ((),...]
    psum x1 -> x0, waiting for transfers between devices: 30.5 us -> none  [spread(): return lax.psum(kept, axis)]
    dot_general x3 -> x0, matrix products: 16 us -> none  [the longest x1 7.37 us: on_device(): jnp.dot(held_block, whole_direction, preferred_element_type=jnp.float32)]
    all_gather x1 -> x0, waiting for transfers between devices: 12.9 us -> none  [on_device(): whole_direction = lax.all_gather(direction, 'dp', axis=0, tiled=True)]
    unnamed x6 -> x7, local copies, waits for them, and re-layouts: 1.14 us -> 5.73 us
  transfers between devices with their start and end apart: 3 -> 0, of which waited for: 3 -> 0; matrix products, arithmetic and copies ran while one was open for 1% -> 0% of each run, Pallas kernels for 0% -> 0%
where the time goes in v1:
time: 121 us; the launch traced here: 120 us
  Pallas kernels  114 us (94%)
  local copies, waits for them, and re-layouts  5.73 us (5%)
    pallas_call x1, Pallas kernels, on_device(): pl.pallas_call(kernel, out_shape=(jax.ShapeDtypeStruct(weight.shape, F32)...  114 us
    unnamed x7, local copies, waits for them, and re-layouts  5.73 us

profile of v1, /device:TPU:1, one launch (start us, length us, event | category | flops | bytes accessed | tf_op | source)
XLA Modules:
  0.0 120.2 jit_solution(18257003896768181988)
XLA Ops:
  0.6 113.8 %shard_map.85 = (f32[512,1792]{1,0:T(8,128)}, f32[64,1792]{1,0:T(8,128)}, f32[64,1792]{1,0:T(8,128)}) custom-call(bf16[512,512]{1,0:T(8,128)(2,1)} %tokens.1, bf16[16,32,1792]{2,1,0:T(8,128)(2,1)} %bitcast.1, bf16[512,1024]{1,0:T(8,128)(2,1)} %projector.1, f32[512,1792]{1,0:T(8,128)} %weight.1, f32[64,1792]{1,0:T(8,128)} %first.1, f32[64,1792]{1,0:T(8,128)} %second.1), custom_call_target="tpu_custom_call" | custom-call | flops 6000000000 | bytes 13631488 | tf_op jit(solution)/shard_map/pallas_call | solution.py:404
  114.4 0.0 copy-start.1
  114.4 0.0 copy-start
  114.4 4.2 %copy.12 = f32[512,1792]{1,0:T(8,128)} copy(f32[512,1792]{1,0:T(8,128)} %get-tuple-element.6) | data formatting | bytes 7340032
  118.6 0.0 copy-done.1
  118.6 0.8 copy.13
  119.4 0.0 copy-done
  119.4 0.8 copy.14
Async XLA Ops:
  114.4 4.2 %copy-start.1 = (f32[64,1792]{1,0:T(8,128)S(1)}, f32[64,1792]{1,0:T(8,128)}, u32[]{:S(2)}) copy-start(f32[64,1792]{1,0:T(8,128)} %get-tuple-element.7) | copy-start | bytes 1376260
  114.4 5.0 %copy-start = (f32[64,1792]{1,0:T(8,128)S(1)}, f32[64,1792]{1,0:T(8,128)}, u32[]{:S(2)}) copy-start(f32[64,1792]{1,0:T(8,128)} %get-tuple-element.8) | copy-start | bytes 1376260

commit v2 on v1

--- a/solution.py
+++ b/solution.py
@@ -17,9 +17,15 @@
 NR = NZ * RB
 FFL = 1792
 HALF = FFL // 2
-TILE = 256
-OFFSET = 2
 PEERS = NY * NX
+
+ORDER = (
+    (0, 0), (0, 1), (0, 2), (0, 3), (1, 0), (1, 1), (1, 2), (1, 3), (2, 0), (2, 1), (2, 2), (2, 3), "scatter",
+    (3, 0), (3, 1), (4, 0), (3, 2), (4, 1), (5, 0), (3, 3), (4, 2), (5, 1), (6, 0), (4, 3), "gather", (5, 2),
+    (6, 1), (7, 0), (5, 3), (6, 2), (7, 1), (8, 0), (6, 3), (7, 2), (8, 1), (9, 0), (7, 3), "held", (8, 2),
+    (9, 1), (10, 0), (8, 3), (9, 2), (10, 1), (11, 0), (12, 0), (9, 3), (10, 2), (11, 1), (12, 1), (10, 3),
+    (11, 2), (12, 2), (11, 3), (12, 3),
+)
 
 
 def kernel(
@@ -48,6 +54,12 @@
             device_id=device, device_id_type=MESH,
         )
 
+    drains = []
+
+    def start(copy):
+        copy.start()
+        drains.append(copy.wait_send)
+
     barrier = pltpu.get_barrier_semaphore()
     for dz in (1, -1):
         pl.semaphore_signal(barrier, inc=1, device_id=at(dz), device_id_type=MESH)
@@ -68,14 +80,14 @@
     for copy in loads:
         copy.start()
 
+    col = lax.broadcasted_iota(jnp.int32, (1, K * NR), 1)
+    natural = col // RB % NZ * (2 * ROWS) + col // NR * RB + col % RB
+
     @pl.loop(0, NZ)
     def _(b):
         row = lax.broadcasted_iota(jnp.int32, (2 * ROWS, K * NR), 0)
-        col = lax.broadcasted_iota(jnp.int32, (2 * ROWS, K * NR), 1)
-        chunk, in_chunk = col // NR, col % NR
-        plane, r = in_chunk // RB, in_chunk % RB
         for cc in range(2):
-            hit = (plane == b) & (row == cc * ROWS + chunk * RB + r)
+            hit = row == natural + (cc * ROWS - b * (2 * ROWS))
             pick[cc, pl.ds(pl.multiple_of(b * 2 * ROWS, 2 * ROWS), 2 * ROWS), :] = jnp.where(
                 hit, 1.0, 0.0
             ).astype(BF16)
@@ -85,20 +97,17 @@
     loads[1].wait()
 
     def partial_product(h):
-        @pl.loop(0, NY)
-        def _(yy):
-            rows = pl.ds(pl.multiple_of(yy * 128, 128), 128)
-            value = jnp.dot(tok_v[h, rows, :], pc[...], preferred_element_type=F32)
-            for k in range(K):
-                part[k, h, yy] = value[:, k * NR : (k + 1) * NR].reshape(NX, 32, NR)
+        value = jnp.dot(tok_v[h], pc[...], preferred_element_type=F32)
+        for k in range(K):
+            part[k, h] = value[:, k * NR : (k + 1) * NR].reshape(NY, NX, 32, NR)
 
     partial_product(c)
 
     pl.semaphore_wait(barrier, 2 + 1 + PEERS - 1)
     tok_copy = remote(tok_v.at[c], tok_v.at[c], tok_sem, 0, sibling)
     go_copy = remote(grad_out, go_v.at[:, c], go_sem, 0, sibling)
-    tok_copy.start()
-    go_copy.start()
+    start(tok_copy)
+    start(go_copy)
 
     def x1(k, h, i):
         if h == 0:
@@ -145,7 +154,7 @@
     def stage_x1(k):
         for h in range(2):
             for i in (1, 2, 3):
-                x1(k, h, i).start()
+                start(x1(k, h, i))
 
     def stage_x2(k):
         for h in range(2):
@@ -154,7 +163,7 @@
             own = part[k, 0, :, pl.ds(x, 1)].reshape(NY, 32, NR) if h == 0 else part[k, 1, y]
             s1[k, h] = own + r1[k, h, 0] + r1[k, h, 1] + r1[k, h, 2]
             for i in (1, 2, 3):
-                x2(k, h, i).start()
+                start(x2(k, h, i))
 
     def stage_pg(k):
         for h in range(2):
@@ -167,6 +176,13 @@
         def _(j):
             plane_gather(k, j).start()
 
+        def drain():
+            @pl.loop(1, PEERS)
+            def _(j):
+                plane_gather(k, j).wait_send()
+
+        drains.append(drain)
+
     def stage_grad(k):
         @pl.loop(1, PEERS)
         def _(j):
@@ -177,19 +193,14 @@
             go_copy.wait_recv()
         pjt[...] = pj[k].reshape(PEERS * 64, NR).T
 
-        @pl.loop(0, FFL // TILE)
-        def _(n):
-            cols = pl.ds(pl.multiple_of(n * TILE, TILE), TILE)
-            value = jnp.dot(
-                pjt[...], go_v[:, :, :, cols].reshape(PEERS * 64, TILE), preferred_element_type=F32
-            )
-            gp[k, :, :, cols] = value.reshape(NZ, RB, TILE)
+        value = jnp.dot(pjt[...], go_v[...].reshape(PEERS * 64, FFL), preferred_element_type=F32)
+        gp[k] = value.reshape(NZ, RB, FFL)
 
         for d in range(2):
             far = lax.rem(z + 4, NZ)
             cols = slice(d * HALF, (d + 1) * HALF)
             zs[k, d, 0, :, cols] = gp[k, far, :, cols].astype(BF16)
-            z_step(k, d, 0).start()
+            start(z_step(k, d, 0))
 
     def stage_z(k, s):
         for d in range(2):
@@ -204,7 +215,7 @@
                 zs[k, d, 1, :, rest] = gp[k, dest, :, rest].astype(BF16)
             else:
                 zs[k, d, s] = (gp[k, dest] + zr[k, d, s - 1].astype(F32)).astype(BF16)
-            z_step(k, d, s).start()
+            start(z_step(k, d, s))
 
     def stage_adam(k):
         for d in range(2):
@@ -224,33 +235,30 @@
             new_first / first_fix / (jnp.sqrt(new_second / second_fix) + 1e-08)
         ).astype(BF16)
         for d in range(2):
-            a_step(k, d, 0).start()
-        sib(k, 0).start()
+            start(a_step(k, d, 0))
+        start(sib(k, 0))
 
     def stage_a(k, s):
         for d in range(2):
             a_step(k, d, s - 1).wait_recv()
-            a_step(k, d, s).start()
-            sib(k, s if d == 0 else NZ - s).start()
+            start(a_step(k, d, s))
+            start(sib(k, s if d == 0 else NZ - s))
 
     def stage_last(k):
         for d in range(2):
             a_step(k, d, 3).wait_recv()
-        sib(k, 4).start()
+        start(sib(k, 4))
 
     def stage_product(k):
         for n in range(NZ):
             sib(k, n).wait_recv()
 
-        @pl.loop(0, FFL // TILE)
-        def _(n):
-            cols = pl.ds(pl.multiple_of(n * TILE, TILE), TILE)
-            value = jnp.dot(
-                hp[:, k * 2 * NR : (k + 1) * 2 * NR],
-                dir_v[k, :, :, :, cols].reshape(2 * NR, TILE),
-                preferred_element_type=F32,
-            )
-            out_w[:, cols] = out_w[:, cols] - 0.5 * value
+        value = jnp.dot(
+            hp[:, k * 2 * NR : (k + 1) * 2 * NR],
+            dir_v[k].reshape(2 * NR, FFL),
+            preferred_element_type=F32,
+        )
+        out_w[...] = out_w[...] - 0.5 * value
 
     holder = dp
     is_holder = t == holder
@@ -280,6 +288,15 @@
             def _(j):
                 scatter(lax.rem(t + j, PEERS)).start()
 
+        def drain():
+            @pl.when(is_holder)
+            def _():
+                @pl.loop(1, PEERS)
+                def _(j):
+                    scatter(lax.rem(t + j, PEERS)).wait_send()
+
+        drains.append(drain)
+
     def stage_held_gather():
         @pl.when(is_holder)
         def _():
@@ -294,6 +311,15 @@
             @pl.when(plane_peer(j)[1] != holder)
             def _():
                 held_gather(j).start()
+
+        def drain():
+            @pl.loop(1, PEERS)
+            def _(j):
+                @pl.when(plane_peer(j)[1] != holder)
+                def _():
+                    held_gather(j).wait_send()
+
+        drains.append(drain)
 
     def stage_held():
         @pl.when(jnp.logical_not(is_holder))
@@ -327,46 +353,15 @@
         functools.partial(lambda s, k: stage_a(k, s), 3),
         stage_last, stage_product,
     ]
-    for slot in range(len(stages) + OFFSET * (K - 1)):
-        if slot == 5:
-            stage_scatter()
-        if slot == 8:
-            stage_held_gather()
-        if slot == 11:
-            stage_held()
-        for k in range(K):
-            n = slot - OFFSET * k
-            if 0 <= n < len(stages):
-                stages[n](k)
-
-    tok_copy.wait_send()
-    go_copy.wait_send()
-    for k in range(K):
-        for h in range(2):
-            for i in (1, 2, 3):
-                x1(k, h, i).wait_send()
-                x2(k, h, i).wait_send()
-            for s in range(4):
-                z_step(k, h, s).wait_send()
-                a_step(k, h, s).wait_send()
-        for n in range(NZ):
-            sib(k, n).wait_send()
-
-        @pl.loop(1, PEERS)
-        def _(j):
-            plane_gather(k, j).wait_send()
-
-    @pl.loop(1, PEERS)
-    def _(j):
-        @pl.when(plane_peer(j)[1] != holder)
-        def _():
-            held_gather(j).wait_send()
-
-    @pl.when(is_holder)
-    def _():
-        @pl.loop(1, PEERS)
-        def _(j):
-            scatter(lax.rem(t + j, PEERS)).wait_send()
+    held_stages = {"scatter": stage_scatter, "gather": stage_held_gather, "held": stage_held}
+    for item in ORDER:
+        if isinstance(item, str):
+            held_stages[item]()
+        else:
+            stages[item[0]](item[1])
+
+    for drain in drains:
+        drain()
 
 
 def on_device(tokens, grad_out, projector, weight, first_moment, second_moment):
@@ -404,15 +399,15 @@
     return pl.pallas_call(
         kernel,
         out_shape=(
-            jax.ShapeDtypeStruct(weight.shape, F32),
-            jax.ShapeDtypeStruct(first_moment.shape, F32),
-            jax.ShapeDtypeStruct(second_moment.shape, F32),
+            pltpu.VMEM(weight.shape, F32),
+            pltpu.VMEM(first_moment.shape, F32),
+            pltpu.VMEM(second_moment.shape, F32),
         ),
         in_specs=[any_spec] * 6,
         out_specs=[vmem_spec] * 3,
         scratch_shapes=scratch,
         compiler_params=pltpu.CompilerParams(
-            collective_id=0, has_side_effects=True, vmem_limit_bytes=56 * 2**20
+            collective_id=0, has_side_effects=True, vmem_limit_bytes=50 * 2**20
         ),
         cost_estimate=pl.CostEstimate(
             flops=6 * 10**9, bytes_accessed=13 * 2**20, transcendentals=0

time: 121 us -> 90.2 us (0.75)
  Pallas kernels: 114 us -> 86.1 us
  local copies, waits for them, and re-layouts: 5.73 us -> 3.37 us
    pallas_call x1, Pallas kernels: 114 us -> 86.1 us  [on_device(): pl.pallas_call(kernel, out_shape=(pltpu.VMEM(weight.shape, F32), pltpu.VM...]
    unnamed x7 -> x3, local copies, waits for them, and re-layouts: 5.73 us -> 3.37 us
where the time goes in v2:
time: 90.2 us; the launch traced here: 90.1 us
  Pallas kernels  86.1 us (95%)
  local copies, waits for them, and re-layouts  3.37 us (4%)
    pallas_call x1, Pallas kernels, on_device(): pl.pallas_call(kernel, out_shape=(pltpu.VMEM(weight.shape, F32), pltpu.VM...  86.1 us
    unnamed x3, local copies, waits for them, and re-layouts  3.37 us

profile of v2, /device:TPU:1, one launch (start us, length us, event | category | flops | bytes accessed | tf_op | source)
XLA Modules:
  0.0 90.1 jit_solution(8365366729840639561)
XLA Ops:
  0.6 86.1 %shard_map.85 = (f32[512,1792]{1,0:T(8,128)S(1)}, f32[64,1792]{1,0:T(8,128)S(1)}, f32[64,1792]{1,0:T(8,128)S(1)}) custom-call(bf16[512,512]{1,0:T(8,128)(2,1)} %tokens.1, bf16[16,32,1792]{2,1,0:T(8,128)(2,1)} %bitcast.1, bf16[512,1024]{1,0:T(8,128)(2,1)} %projector.1, f32[512,1792]{1,0:T(8,128)} %weight.1, f32[64,1792]{1,0:T(8,128)} %first.1, f32[64,1792]{1,0:T(8,128)} %second.1), custom_call_target="tpu_custom_call" | custom-call | flops 6000000000 | bytes 13631488 | tf_op jit(solution)/shard_map/pallas_call | solution.py:399
  86.7 1.8 %copy.12 = f32[512,1792]{1,0:T(8,128)} copy(f32[512,1792]{1,0:T(8,128)S(1)} %get-tuple-element.3) | data formatting | bytes 7340032
  88.6 0.8 copy.13
  89.3 0.8 copy.14

commit v3 on v2

--- a/solution.py
+++ b/solution.py
@@ -17,14 +17,15 @@
 NR = NZ * RB
 FFL = 1792
 HALF = FFL // 2
+FAR = ((pl.ds(0, 512), pl.ds(512, 384)), (pl.ds(896, 384), pl.ds(1280, 512)))
 PEERS = NY * NX
 
 ORDER = (
-    (0, 0), (0, 1), (0, 2), (0, 3), (1, 0), (1, 1), (1, 2), (1, 3), (2, 0), (2, 1), (2, 2), (2, 3), "scatter",
-    (3, 0), (3, 1), (4, 0), (3, 2), (4, 1), (5, 0), (3, 3), (4, 2), (5, 1), (6, 0), (4, 3), "gather", (5, 2),
-    (6, 1), (7, 0), (5, 3), (6, 2), (7, 1), (8, 0), (6, 3), (7, 2), (8, 1), (9, 0), (7, 3), "held", (8, 2),
-    (9, 1), (10, 0), (8, 3), (9, 2), (10, 1), (11, 0), (12, 0), (9, 3), (10, 2), (11, 1), (12, 1), (10, 3),
-    (11, 2), (12, 2), (11, 3), (12, 3),
+    (0, 0), (0, 1), (0, 2), "tok", "pp", (1, 0), (1, 2), "go", (1, 1), (2, 0), (1, 3), (0, 3), (2, 1), (2, 2),
+    (3, 0), (2, 3), (3, 1), (3, 2), (4, 0), (3, 3), (4, 1), "scatter", (5, 0), (4, 2), (5, 1), (6, 0), (4, 3),
+    (5, 2), (6, 1), (5, 3), (6, 2), "gather", (7, 1), (7, 0), (6, 3), (7, 2), (8, 1), (7, 3), (8, 0), (8, 2),
+    (9, 1), (8, 3), (9, 2), (10, 1), (9, 0), (9, 3), (10, 2), (11, 1), (10, 0), "held", (10, 3), (12, 1),
+    (11, 2), (11, 0), (11, 3), (12, 2), (13, 1), (12, 0), (13, 2), (12, 3), (13, 0), (13, 3),
 )
 
 
@@ -54,7 +55,7 @@
             device_id=device, device_id_type=MESH,
         )
 
-    drains = []
+    drains, seen = [], set()
 
     def start(copy):
         copy.start()
@@ -106,8 +107,6 @@
     pl.semaphore_wait(barrier, 2 + 1 + PEERS - 1)
     tok_copy = remote(tok_v.at[c], tok_v.at[c], tok_sem, 0, sibling)
     go_copy = remote(grad_out, go_v.at[:, c], go_sem, 0, sibling)
-    start(tok_copy)
-    start(go_copy)
 
     def x1(k, h, i):
         if h == 0:
@@ -134,27 +133,51 @@
     def plane_gather(k, j):
         return remote(pj.at[k, t], pj.at[k, t], pg_sem, k * PEERS + j, plane_peer(j))
 
-    def z_step(k, d, s):
-        cols = pl.ds(d * HALF, HALF) if s == 0 else pl.ds(0, FFL)
+    def columns(q, s, far_step, d):
+        return FAR[q][d] if s == far_step else pl.ds(q * HALF, HALF)
+
+    def z_step(k, d, s, q):
+        cols = columns(q, s, 0, d)
         return remote(
-            zs.at[k, d, s, :, cols], zr.at[k, d, s, :, cols], z_sem, (k * 2 + d) * 4 + s,
+            zs.at[k, d, s, :, cols], zr.at[k, d, s, :, cols], z_sem, ((k * 2 + d) * 4 + s) * 2 + q,
             at(1 if d == 0 else -1),
         )
 
-    def a_step(k, d, s):
+    def a_step(k, d, s, q):
         piece = lax.rem(z + (NZ - s if d == 0 else s), NZ)
-        cols = pl.ds(d * HALF, HALF) if s == 3 else pl.ds(0, FFL)
-        ref = dir_v.at[k, c, piece, :, cols]
-        return remote(ref, ref, a_sem, (k * 2 + d) * 4 + s, at(1 if d == 0 else -1))
+        ref = dir_v.at[k, c, piece, :, columns(q, s, 3, d)]
+        return remote(ref, ref, a_sem, ((k * 2 + d) * 4 + s) * 2 + q, at(1 if d == 0 else -1))
 
     def sib(k, n):
         ref = dir_v.at[k, c, lax.rem(z + NZ - n, NZ)]
         return remote(ref, ref, sib_sem, k * NZ + n, sibling)
 
-    def stage_x1(k):
+    def send_half(k, core_of_half):
         for h in range(2):
+            @pl.when(core_of_half == h)
+            def _():
+                for i in (1, 2, 3):
+                    x1(k, h, i).start()
+
             for i in (1, 2, 3):
-                start(x1(k, h, i))
+                if core_of_half is c:
+                    drains.append(x1(k, h, i).wait_send)
+
+    def stage_own_half(k):
+        send_half(k, c)
+
+    def stage_other_half(k):
+        send_half(k, 1 - c)
+
+    def stage_swap_tokens():
+        start(tok_copy)
+
+    def stage_other_partial():
+        tok_copy.wait_recv()
+        partial_product(1 - c)
+
+    def stage_swap_grad():
+        start(go_copy)
 
     def stage_x2(k):
         for h in range(2):
@@ -188,7 +211,8 @@
         def _(j):
             plane_gather(k, j).wait_recv()
 
-        if k == 0:
+        if "grad" not in seen:
+            seen.add("grad")
             loads[2].wait()
             go_copy.wait_recv()
         pjt[...] = pj[k].reshape(PEERS * 64, NR).T
@@ -196,57 +220,69 @@
         value = jnp.dot(pjt[...], go_v[...].reshape(PEERS * 64, FFL), preferred_element_type=F32)
         gp[k] = value.reshape(NZ, RB, FFL)
 
-        for d in range(2):
-            far = lax.rem(z + 4, NZ)
-            cols = slice(d * HALF, (d + 1) * HALF)
-            zs[k, d, 0, :, cols] = gp[k, far, :, cols].astype(BF16)
-            start(z_step(k, d, 0))
+        far = lax.rem(z + 4, NZ)
+        for q in range(2):
+            for d in range(2):
+                cols = FAR[q][d]
+                zs[k, d, 0, :, cols] = gp[k, far, :, cols].astype(BF16)
+                start(z_step(k, d, 0, q))
 
     def stage_z(k, s):
-        for d in range(2):
-            z_step(k, d, s - 1).wait_recv()
-            dest = lax.rem(z + (4 - s if d == 0 else NZ - 4 + s), NZ)
-            if s == 1:
-                got = slice(d * HALF, (d + 1) * HALF)
-                rest = slice((1 - d) * HALF, (2 - d) * HALF)
-                zs[k, d, 1, :, got] = (
-                    gp[k, dest, :, got] + zr[k, d, 0, :, got].astype(F32)
-                ).astype(BF16)
-                zs[k, d, 1, :, rest] = gp[k, dest, :, rest].astype(BF16)
-            else:
-                zs[k, d, s] = (gp[k, dest] + zr[k, d, s - 1].astype(F32)).astype(BF16)
-            start(z_step(k, d, s))
+        for q in range(2):
+            half = pl.ds(q * HALF, HALF)
+            for d in range(2):
+                z_step(k, d, s - 1, q).wait_recv()
+                dest = lax.rem(z + (4 - s if d == 0 else NZ - 4 + s), NZ)
+                if s == 1:
+                    got, rest = FAR[q][d], FAR[q][1 - d]
+                    zs[k, d, 1, :, got] = (
+                        gp[k, dest, :, got] + zr[k, d, 0, :, got].astype(F32)
+                    ).astype(BF16)
+                    zs[k, d, 1, :, rest] = gp[k, dest, :, rest].astype(BF16)
+                else:
+                    zs[k, d, s, :, half] = (
+                        gp[k, dest, :, half] + zr[k, d, s - 1, :, half].astype(F32)
+                    ).astype(BF16)
+                start(z_step(k, d, s, q))
 
     def stage_adam(k):
-        for d in range(2):
-            z_step(k, d, 3).wait_recv()
-        if k == 0:
+        if "adam" not in seen:
+            seen.add("adam")
             loads[3].wait()
             loads[4].wait()
         rows = slice(k * RB, (k + 1) * RB)
-        grad = gp[k, z] + zr[k, 0, 3].astype(F32) + zr[k, 1, 3].astype(F32)
-        new_first = 0.9 * first_v[rows, :] + 0.1 * grad
-        new_second = 0.999 * second_v[rows, :] + 0.001 * grad * grad
-        out_first[rows, :] = new_first
-        out_second[rows, :] = new_second
         first_fix = 1.0 - 0.9**STEP
         second_fix = 1.0 - 0.999**STEP
-        dir_v[k, c, z] = (
-            new_first / first_fix / (jnp.sqrt(new_second / second_fix) + 1e-08)
-        ).astype(BF16)
-        for d in range(2):
-            start(a_step(k, d, 0))
+        for q in range(2):
+            half = pl.ds(q * HALF, HALF)
+            for d in range(2):
+                z_step(k, d, 3, q).wait_recv()
+            grad = (
+                gp[k, z, :, half] + zr[k, 0, 3, :, half].astype(F32) + zr[k, 1, 3, :, half].astype(F32)
+            )
+            new_first = 0.9 * first_v[rows, half] + 0.1 * grad
+            new_second = 0.999 * second_v[rows, half] + 0.001 * grad * grad
+            out_first[rows, half] = new_first
+            out_second[rows, half] = new_second
+            dir_v[k, c, z, :, half] = (
+                new_first / first_fix / (jnp.sqrt(new_second / second_fix) + 1e-08)
+            ).astype(BF16)
+            for d in range(2):
+                start(a_step(k, d, 0, q))
         start(sib(k, 0))
 
     def stage_a(k, s):
-        for d in range(2):
-            a_step(k, d, s - 1).wait_recv()
-            start(a_step(k, d, s))
-            start(sib(k, s if d == 0 else NZ - s))
+        for q in range(2):
+            for d in range(2):
+                a_step(k, d, s - 1, q).wait_recv()
+                start(a_step(k, d, s, q))
+        for n in (s, NZ - s):
+            start(sib(k, n))
 
     def stage_last(k):
-        for d in range(2):
-            a_step(k, d, 3).wait_recv()
+        for q in range(2):
+            for d in range(2):
+                a_step(k, d, 3, q).wait_recv()
         start(sib(k, 4))
 
     def stage_product(k):
@@ -329,21 +365,15 @@
                 held_gather(j).wait_recv()
 
         for cc in range(2):
-            @pl.loop(0, 4)
-            def _(b):
-                rows = pl.ds(pl.multiple_of(b * 128, 128), 128)
-                value = jnp.dot(held[rows, :], pick[cc], preferred_element_type=F32).astype(BF16)
-                for k in range(K):
-                    lo = (k * 2 + cc) * NR
-                    hp[rows, lo : lo + NR] = value[:, k * NR : (k + 1) * NR]
+            value = jnp.dot(held[...], pick[cc], preferred_element_type=F32).astype(BF16)
+            for k in range(K):
+                lo = (k * 2 + cc) * NR
+                hp[:, lo : lo + NR] = value[:, k * NR : (k + 1) * NR]
 
         loads[5].wait()
 
-    tok_copy.wait_recv()
-    partial_product(1 - c)
-
     stages = [
-        stage_x1, stage_x2, stage_pg, stage_grad,
+        stage_own_half, stage_other_half, stage_x2, stage_pg, stage_grad,
         functools.partial(lambda s, k: stage_z(k, s), 1),
         functools.partial(lambda s, k: stage_z(k, s), 2),
         functools.partial(lambda s, k: stage_z(k, s), 3),
@@ -353,10 +383,13 @@
         functools.partial(lambda s, k: stage_a(k, s), 3),
         stage_last, stage_product,
     ]
-    held_stages = {"scatter": stage_scatter, "gather": stage_held_gather, "held": stage_held}
+    once = {
+        "tok": stage_swap_tokens, "pp": stage_other_partial, "go": stage_swap_grad,
+        "scatter": stage_scatter, "gather": stage_held_gather, "held": stage_held,
+    }
     for item in ORDER:
         if isinstance(item, str):
-            held_stages[item]()
+            once[item]()
         else:
             stages[item[0]](item[1])
 
@@ -391,7 +424,7 @@
         pltpu.VMEM((512, 1024), BF16),
         pltpu.VMEM((512, 1024), BF16),
         dma((7,)),
-        pair(1), pair(1), pair(K * 6), pair(K * 6), pair(K * PEERS), pair(K * 8), pair(K * 8),
+        pair(1), pair(1), pair(K * 6), pair(K * 6), pair(K * PEERS), pair(K * 16), pair(K * 16),
         pair(K * NZ), pair(PEERS), pair(PEERS),
     ]
     any_spec = pl.BlockSpec(memory_space=pl.ANY)

time: 90.2 us -> 86.3 us (0.957)
  Pallas kernels: 86.1 us -> 82.3 us
    pallas_call x1, Pallas kernels: 86.1 us -> 82.3 us  [on_device(): pl.pallas_call(kernel, out_shape=(pltpu.VMEM(weight.shape, F32), pltpu.VM...]
where the time goes in v3:
time: 86.3 us
  Pallas kernels  82.3 us (95%)
  local copies, waits for them, and re-layouts  3.37 us (4%)
    pallas_call x1, Pallas kernels, on_device(): pl.pallas_call(kernel, out_shape=(pltpu.VMEM(weight.shape, F32), pltpu.VM...  82.3 us
    unnamed x3, local copies, waits for them, and re-layouts  3.37 us

profile of v3, /device:TPU:1, one launch (start us, length us, event | category | flops | bytes accessed | tf_op | source)
XLA Modules:
  0.0 86.3 jit_solution(10148889176784653856)
XLA Ops:
  0.6 82.3 %shard_map.85 = (f32[512,1792]{1,0:T(8,128)S(1)}, f32[64,1792]{1,0:T(8,128)S(1)}, f32[64,1792]{1,0:T(8,128)S(1)}) custom-call(bf16[512,512]{1,0:T(8,128)(2,1)} %tokens.1, bf16[16,32,1792]{2,1,0:T(8,128)(2,1)} %bitcast.1, bf16[512,1024]{1,0:T(8,128)(2,1)} %projector.1, f32[512,1792]{1,0:T(8,128)} %weight.1, f32[64,1792]{1,0:T(8,128)} %first.1, f32[64,1792]{1,0:T(8,128)} %second.1), custom_call_target="tpu_custom_call" | custom-call | flops 6000000000 | bytes 13631488 | tf_op jit(solution)/shard_map/pallas_call | solution.py:432
  82.9 1.8 %copy.12 = f32[512,1792]{1,0:T(8,128)} copy(f32[512,1792]{1,0:T(8,128)S(1)} %get-tuple-element.3) | data formatting | bytes 7340032
  84.7 0.8 copy.13
  85.5 0.8 copy.14

commit v4 on v3

--- a/solution.py
+++ b/solution.py
@@ -17,6 +17,8 @@
 NR = NZ * RB
 FFL = 1792
 HALF = FFL // 2
+LAST = 3
+BLOCKS = 4
 FAR = ((pl.ds(0, 512), pl.ds(512, 384)), (pl.ds(896, 384), pl.ds(1280, 512)))
 PEERS = NY * NX
 
@@ -24,16 +26,16 @@
     (0, 0), (0, 1), (0, 2), "tok", "pp", (1, 0), (1, 2), "go", (1, 1), (2, 0), (1, 3), (0, 3), (2, 1), (2, 2),
     (3, 0), (2, 3), (3, 1), (3, 2), (4, 0), (3, 3), (4, 1), "scatter", (5, 0), (4, 2), (5, 1), (6, 0), (4, 3),
     (5, 2), (6, 1), (5, 3), (6, 2), "gather", (7, 1), (7, 0), (6, 3), (7, 2), (8, 1), (7, 3), (8, 0), (8, 2),
-    (9, 1), (8, 3), (9, 2), (10, 1), (9, 0), (9, 3), (10, 2), (11, 1), (10, 0), "held", (10, 3), (12, 1),
-    (11, 2), (11, 0), (11, 3), (12, 2), (13, 1), (12, 0), (13, 2), (12, 3), (13, 0), (13, 3),
+    (9, 1), (8, 3), (9, 2), (10, 1), (9, 0), (9, 3), (10, 2), (11, 1), (10, 0), (10, 3), (12, 1), (11, 2),
+    (11, 0), (11, 3), "held", (12, 2), (13, 1), (12, 0), (13, 2), (12, 3), (13, 0), (13, 3),
 )
 
 
 def kernel(
     tokens, grad_out, projector, weight, first, second,
-    out_w, out_first, out_second,
+    out_w, out_first, out_second, dir_v, hp,
     tok_v, go_v, proj_v, first_v, second_v, pick, pc, part, r1, s1, r2, pj, pjt, gp,
-    zs, zr, dir_v, held, hp,
+    zs, zr, held,
     load_sem, tok_sem, go_sem, x1_sem, x2_sem, pg_sem, z_sem, a_sem, sib_sem, sc_sem, hg_sem,
 ):
     dp, t = lax.axis_index("dp"), lax.axis_index("tensor")
@@ -288,6 +290,8 @@
     def stage_product(k):
         for n in range(NZ):
             sib(k, n).wait_recv()
+        if k == LAST:
+            return
 
         value = jnp.dot(
             hp[:, k * 2 * NR : (k + 1) * 2 * NR],
@@ -397,6 +401,29 @@
         drain()
 
 
+def finish(weight, first, second, dir_v, hp, out_w, out_first, out_second, done, sem):
+    copies = [
+        pltpu.make_async_copy(first, out_first, sem.at[BLOCKS]),
+        pltpu.make_async_copy(second, out_second, sem.at[BLOCKS + 1]),
+    ]
+    for copy in copies:
+        copy.start()
+    size = weight.shape[0] // BLOCKS
+    for b in range(BLOCKS):
+        rows = pl.ds(b * size, size)
+        value = jnp.dot(
+            hp[rows, LAST * 2 * NR : (LAST + 1) * 2 * NR],
+            dir_v[LAST].reshape(2 * NR, FFL),
+            preferred_element_type=F32,
+        )
+        done[rows, :] = weight[rows, :] - 0.5 * value
+        copy = pltpu.make_async_copy(done.at[rows], out_w.at[rows], sem.at[b])
+        copy.start()
+        copies.append(copy)
+    for copy in copies:
+        copy.wait()
+
+
 def on_device(tokens, grad_out, projector, weight, first_moment, second_moment):
     dma = pltpu.SemaphoreType.DMA
 
@@ -420,8 +447,6 @@
         pltpu.VMEM((K, NZ, RB, FFL), F32),
         pltpu.VMEM((K, 2, 4, RB, FFL), BF16),
         pltpu.VMEM((K, 2, 4, RB, FFL), BF16),
-        pltpu.VMEM((K, 2, NZ, RB, FFL), BF16),
-        pltpu.VMEM((512, 1024), BF16),
         pltpu.VMEM((512, 1024), BF16),
         dma((7,)),
         pair(1), pair(1), pair(K * 6), pair(K * 6), pair(K * PEERS), pair(K * 16), pair(K * 16),
@@ -429,23 +454,38 @@
     ]
     any_spec = pl.BlockSpec(memory_space=pl.ANY)
     vmem_spec = pl.BlockSpec(memory_space=pltpu.VMEM)
-    return pl.pallas_call(
+    values = pl.pallas_call(
         kernel,
         out_shape=(
             pltpu.VMEM(weight.shape, F32),
             pltpu.VMEM(first_moment.shape, F32),
             pltpu.VMEM(second_moment.shape, F32),
+            pltpu.VMEM((K, 2, NZ, RB, FFL), BF16),
+            pltpu.VMEM((512, 1024), BF16),
         ),
         in_specs=[any_spec] * 6,
-        out_specs=[vmem_spec] * 3,
+        out_specs=[vmem_spec] * 5,
         scratch_shapes=scratch,
         compiler_params=pltpu.CompilerParams(
-            collective_id=0, has_side_effects=True, vmem_limit_bytes=50 * 2**20
+            collective_id=0, has_side_effects=True, vmem_limit_bytes=103 * 2**19
         ),
         cost_estimate=pl.CostEstimate(
             flops=6 * 10**9, bytes_accessed=13 * 2**20, transcendentals=0
         ),
     )(tokens, grad_out.reshape(PEERS, 32, FFL), projector, weight, first_moment, second_moment)
+    return pl.pallas_call(
+        finish,
+        out_shape=tuple(
+            jax.ShapeDtypeStruct(a.shape, F32) for a in (weight, first_moment, second_moment)
+        ),
+        in_specs=[vmem_spec] * 5,
+        out_specs=[any_spec] * 3,
+        scratch_shapes=[pltpu.VMEM(weight.shape, F32), dma((BLOCKS + 2,))],
+        compiler_params=pltpu.CompilerParams(vmem_limit_bytes=44 * 2**20),
+        cost_estimate=pl.CostEstimate(
+            flops=470 * 10**6, bytes_accessed=5 * 2**20, transcendentals=0
+        ),
+    )(*values)
 
 
 def solution(mesh):

time: 86.3 us -> 84.4 us (0.978)
  local copies, waits for them, and re-layouts: 3.37 us -> 0 us
  Pallas kernels: 82.3 us -> 83.7 us
    unnamed x3 -> x0, local copies, waits for them, and re-layouts: 3.37 us -> none
    pallas_call x0 -> x1, Pallas kernels: none -> 2.2 us  [on_device(): pl.pallas_call(finish, out_shape=tuple((jax.ShapeDtypeStruct(a.shape, F32...]
where the time goes in v4:
time: 84.4 us; the launch traced here: 84.3 us
  Pallas kernels  83.7 us (99%)
    pallas_call x1, Pallas kernels, on_device(): pl.pallas_call(kernel, out_shape=(pltpu.VMEM(weight.shape, F32), pltpu.VM...  81.5 us
    pallas_call x1, Pallas kernels, on_device(): pl.pallas_call(finish, out_shape=tuple((jax.ShapeDtypeStruct(a.shape, F32...  2.2 us

profile of v4, /device:TPU:1, one launch (start us, length us, event | category | flops | bytes accessed | tf_op | source)
XLA Modules:
  0.0 84.3 jit_solution(7071356247798337049)
XLA Ops:
  0.6 81.5 %shard_map.85 = (f32[512,1792]{1,0:T(8,128)S(1)}, f32[64,1792]{1,0:T(8,128)S(1)}, f32[64,1792]{1,0:T(8,128)S(1)}, bf16[4,2,8,16,1792]{4,3,2,1,0:T(8,128)(2,1)S(1)}, bf16[512,1024]{1,0:T(8,128)(2,1)S(1)}) custom-call(bf16[512,512]{1,0:T(8,128)(2,1)} %tokens.1, bf16[16,32,1792]{2,1,0:T(8,128)(2,1)} %bitcast.1, bf16[512,1024]{1,0:T(8,128)(2,1)} %projector.1, ...), custom_call_target="tpu_custom_call" | custom-call | flops 6000000000 | bytes 13631488 | tf_op jit(solution)/shard_map/pallas_call | solution.py:457
  82.1 2.2 %shard_map.86 = (f32[512,1792]{1,0:T(8,128)}, f32[64,1792]{1,0:T(8,128)}, f32[64,1792]{1,0:T(8,128)}) custom-call(f32[512,1792]{1,0:T(8,128)S(1)} %get-tuple-element.8.weight, f32[64,1792]{1,0:T(8,128)S(1)} %get-tuple-element.9.first, f32[64,1792]{1,0:T(8,128)S(1)} %get-tuple-element.10.second, bf16[4,2,8,16,1792]{4,3,2,1,0:T(8,128)(2,1)S(1)} %get-tuple-element.11.dir_v, ...), custom_call_target="tpu_custom_call" | custom-call | flops 470000000 | bytes 5242880 | tf_op jit(solution)/shard_map/pallas_call | solution.py:476
